TPU v7x, 256 devices: a whole 4x4x8 slice. The times are simulated.
256 devices in a mesh: section: 16 (over y, z_hi), res: 16 (over x, z_lo, core).
Axes of the slice: x: 4, y: 4, z: 8 (z_hi: 4, z_lo: 2; z = z_hi * 2 + z_lo), core: 2. Of those that a mesh axis runs over, the one named last changes fastest.
Arguments:
- normed_sequence_states: bfloat16 [16, 256, 128, 256], P('section', 'res'), may hold values from -6 to 6
- first_factor_tensor: bfloat16 [16, 256, 32], P('section'), may hold values from -0.375 to 0.375
- second_factor_tensor: bfloat16 [16, 256, 32], P('section'), may hold values from -0.375 to 0.375
- output_projection_weight: bfloat16 [16, 1024, 128], P('section'), may hold values from -0.1875 to 0.1875
- pair_external_gradient: bfloat16 [16, 256, 256, 128], P('section', 'res'), may hold values from -48 to 48
- pair_channel_gains: float32 [16, 128], P('section'), may hold values from 0.05 to 1
Outputs:
- msa_grad: bfloat16 [16, 256, 128, 256], P('section', 'res')
All inputs are finite; a program needn't handle non-finite values.
Results may differ from a plain program's by a relative error of at most 0.02.
Values may be sent and summed in bfloat16 or wider, within the bound.
A program may use at most 192 MiB of HBM per device.

v0:
```python
import jax
import jax.numpy as jnp
from jax import lax
from jax.sharding import PartitionSpec as P


def carried_in(value, axis, join, neutral):
    count, mine = (lax.axis_size(axis), lax.axis_index(axis))
    pieces = jax.tree.map(lambda part: lax.all_gather(part, axis), value)
    pieces = jax.tree.map(lambda part: part[::-1], pieces)
    mine = count - 1 - mine
    so_far = jax.tree.map(
        lambda part, zero: jnp.full_like(part, 0) + jnp.asarray(zero, part.dtype), value, neutral
    )

    def turn(position, so_far):
        longer = join(so_far, jax.tree.map(lambda part: part[position], pieces))
        return jax.tree.map(lambda new, old: jnp.where(position < mine, new, old), longer, so_far)

    return lax.fori_loop(0, count - 1, turn, so_far)


def compose(earlier, later):
    return (earlier[0] * later[0], later[0][:, None, None, :] * earlier[1] + later[1])


def shards(
    normed_sequence_states,
    first_factor_tensor,
    second_factor_tensor,
    output_projection_weight,
    pair_external_gradient,
    pair_channel_gains,
):
    grad_in = pair_external_gradient.astype(jnp.float32)
    passed_in = pair_channel_gains[:, None, None, :] * grad_in
    identity = (jnp.ones_like(pair_channel_gains), jnp.zeros_like(passed_in))
    _, from_later = carried_in((pair_channel_gains, passed_in), "section", compose, identity)
    pair_half = (grad_in + from_later)[0].astype(jnp.bfloat16)
    alignment_block_input = normed_sequence_states[0]
    left_weight_matrix = first_factor_tensor[0]
    right_weight_matrix = second_factor_tensor[0]
    weight_out = output_projection_weight[0]
    proj_width = left_weight_matrix.shape[1]
    alignment_row_count = alignment_block_input.shape[1]
    first_factor_vectors = jnp.einsum(
        "egw,wa->eag", alignment_block_input, left_weight_matrix, preferred_element_type=jnp.float32
    ).astype(jnp.bfloat16)
    second_factor_vectors = jnp.einsum(
        "egw,wa->eag",
        alignment_block_input,
        right_weight_matrix,
        preferred_element_type=jnp.float32,
    ).astype(jnp.bfloat16)
    incoming_adjoint = jnp.einsum(
        "ijp,qp->ijq", pair_half, weight_out, preferred_element_type=jnp.float32
    ).astype(jnp.bfloat16)
    incoming_adjoint = incoming_adjoint.reshape(
        incoming_adjoint.shape[0], incoming_adjoint.shape[1], proj_width, proj_width
    )
    columns = incoming_adjoint
    left_gradient_sum = jnp.einsum(
        "zfay,fyb->zab",
        columns,
        lax.all_gather(second_factor_vectors, "res", axis=0, tiled=True),
        preferred_element_type=jnp.float32,
    )
    columns = incoming_adjoint
    right_gradient_sum = lax.psum_scatter(
        jnp.einsum(
            "mvpg,mpw->vgw", columns, first_factor_vectors, preferred_element_type=jnp.float32
        ).astype(jnp.bfloat16),
        "res",
        scatter_dimension=0,
        tiled=True,
    ).astype(jnp.float32)
    first_factor_adjoint = (left_gradient_sum / alignment_row_count).astype(jnp.bfloat16)
    second_factor_adjoint = (right_gradient_sum / alignment_row_count).astype(jnp.bfloat16)
    total = jnp.einsum(
        "ixs,kx->isk", first_factor_adjoint, left_weight_matrix, preferred_element_type=jnp.float32
    )
    total = total + jnp.einsum(
        "ixs,kx->isk",
        second_factor_adjoint,
        right_weight_matrix,
        preferred_element_type=jnp.float32,
    )
    return total.astype(jnp.bfloat16)[None]


def solution(mesh):
    in_specs = (
        P("section", "res", None, None),
        P("section", None, None),
        P("section", None, None),
        P("section", None, None),
        P("section", "res", None, None),
        P("section", None),
    )
    out_specs = P("section", "res", None, None)
    return jax.shard_map(shards, mesh=mesh, in_specs=in_specs, out_specs=out_specs, check_vma=False)
```

profile of v0, /device:TPU:33, one launch (start us, length us, event | category | flops | bytes accessed | tf_op | source)
XLA Modules:
  0.0 619.8 jit_solution(10715444446318957711)
XLA Ops:
  6.5 0.0 copy-start
  6.5 0.0 all-gather.8.cloned.1.call-start
  6.5 0.0 copy-start.3
  6.5 2.9 convert_multiply_fusion
  9.4 0.0 copy-start.4
  9.4 0.0 all-gather.8.cloned.1.call-update
  9.4 0.0 all-gather.6.cloned.1.call-start
  9.5 0.0 copy-done
  9.5 0.0 copy-done.3
  9.5 1.1 fusion.17
  10.6 0.0 all-gather.6.cloned.1.call-update
  10.6 0.0 reduce-scatter.2.cloned.1.call-start
  10.7 0.0 copy-done.4
  10.7 40.8 %all-gather.2 = f32[16,1,128]{2,1,0:T(1,128)S(1)} all-gather(f32[1,1,128]{2,1,0:T(1,128)S(1)} %bitcast.87), channel_id=2, replica_groups=mesh['section'=16,'res'=16] {'section'}, dimensions={0}, use_global_device_ids=true | all-gather | bytes 8704 | tf_op jit(solution)/shard_map/all_gather | solution.py:9
  51.5 332.0 %all-gather.8.cloned.1.call-done = f32[16,16,256,128]{3,2,1,0:T(8,128)} async-done(((f32[1,16,256,128]{3,2,1,0:T(8,128)}), f32[16,16,256,128]{3,2,1,0:T(8,128)}) %all-gather.8.cloned.1.call-update) | async-done | bytes 33554448 | tf_op jit(solution)/shard_map/all_gather | solution.py:9
  383.6 22.9 %reverse_bitcast_fusion = f32[16,1,16,256,128]{4,3,2,1,0:T(8,128)} fusion(f32[16,16,256,128]{3,2,1,0:T(8,128)} %all-gather.8.cloned.1.call-done), kind=kLoop, calls=%fused_computation.3 | loop fusion | bytes 67108864
  406.5 0.0 copy-start.2
  406.5 52.3 %while.14 = (s32[]{:T(128)}, f32[1,16,256,128]{3,2,1,0:T(8,128)S(1)}, s32[]{:T(128)}, f32[16,1,128]{2,1,0:T(1,128)S(1)}, f32[16,1,16,256,128]{4,3,2,1,0:T(8,128)}, /*index=5*/s32[]{:T(128)}, s32[]{:T(128)}) while((s32[]{:T(128)}, f32[1,16,256,128]{3,2,1,0:T(8,128)S(1)}, s32[]{:T(128)}, f32[16,1,128]{2,1,0:T(1,128)S(1)}, ...), condition=%wide.region_1.2_spmd.clone, body=%wide.region_0.1_spmd.clone.sunk | while | flops 2097156 | bytes 6293097 | solution.py:20
  406.5 3.5 fusion.37
  410.1 3.4 fusion.37
  413.5 3.5 fusion.37
  417.0 3.5 fusion.37
  420.5 3.4 fusion.37
  424.0 3.4 fusion.37
  427.5 3.4 fusion.37
  431.0 3.4 fusion.37
  434.5 3.4 fusion.37
  437.9 3.4 fusion.37
  441.4 3.4 fusion.37
  444.9 3.4 fusion.37
  448.4 3.4 fusion.37
  451.9 3.4 fusion.37
  455.4 3.4 fusion.37
  458.8 0.0 copy-done.2
  458.8 6.8 %convolution_convert_fusion = bf16[16,256,1024]{2,1,0:T(8,128)(2,1)} fusion(f32[1,16,256,128]{3,2,1,0:T(8,128)S(1)} %get-tuple-element.99, bf16[1,16,256,128]{3,2,1,0:T(8,128)(2,1)} %param.12, bf16[1,1024,128]{2,1,0:T(8,128)(2,1)S(1)} %copy-done.2), kind=kOutput, calls=%fused_computation.4 | convolution fusion | flops 1079508992 | bytes 11796480 | tf_op jit(solution)/shard_map/ijp,qp->ijq/dot_general | solution.py:55
  465.6 12.2 %copy.21 = bf16[16,256,1024]{1,2,0:T(8,128)(2,1)} copy(bf16[16,256,1024]{2,1,0:T(8,128)(2,1)} %convolution_convert_fusion) | data formatting | bytes 16777216 | tf_op jit(solution)/shard_map/convert_element_type | solution.py:57
  477.8 0.0 copy-start.5
  477.8 55.0 %copy.23 = bf16[16,256,32,32]{2,3,0,1:T(8,128)(2,1)} copy(bf16[16,256,32,32]{1,3,2,0:T(8,128)(2,1)} %bitcast.82) | data formatting | bytes 16777216 | tf_op jit(solution)/shard_map/reshape | solution.py:58
  532.8 0.0 copy-done.5
  532.8 15.6 %bitcast_convert_fusion = bf16[256,32,128]{2,1,0:T(8,128)(2,1)} fusion(bf16[16,256,32,32]{2,3,0,1:T(8,128)(2,1)} %copy.23, bf16[1,16,128,256]{3,2,1,0:T(8,128)(2,1)S(1)} %copy-done, bf16[1,256,32]{1,2,0:T(8,128)(2,1)S(1)} %copy-done.5), kind=kOutput, calls=%fused_computation.5 | convolution fusion | flops 1108410368 | bytes 11550720 | tf_op jit(solution)/shard_map/mvpg,mpw->vgw/dot_general | solution.py:70
  548.4 0.0 reduce-scatter.2.cloned.1.call-update
  548.5 44.2 %copy.22 = bf16[16,256,32,32]{3,2,1,0:T(8,128)(2,1)} copy(bf16[16,256,32,32]{1,3,2,0:T(8,128)(2,1)} %bitcast.83) | data formatting | bytes 16777216 | tf_op jit(solution)/shard_map/reshape | solution.py:58
  592.7 0.0 all-gather.6.cloned.1.call-done
  592.7 0.0 copy-start.1
  592.7 18.2 %fusion.15 = f32[16,128,256]{2,1,0:T(8,128)S(1)} fusion(bf16[16,256,32,32]{3,2,1,0:T(8,128)(2,1)} %copy.22, bf16[256,32,128]{2,1,0:T(8,128)(2,1)} %all-gather.6.cloned.1.call-done, bf16[1,256,32]{1,2,0:T(8,128)(2,1)S(1)} %copy-done.5), kind=kOutput, calls=%fused_computation.18 | convolution fusion | flops 1107427328 | bytes 12599296 | tf_op jit(solution)/shard_map/ixs,kx->isk/dot_general | solution.py:79
  610.9 0.0 reduce-scatter.2.cloned.1.call-done
  610.9 2.4 fusion.4
  613.3 0.0 copy-done.1
  (17 shorter events, 0.1 us)
Async XLA Ops:
  6.5 2.9 copy-start
  6.5 377.0 %all-gather.8.cloned.1.call-start = ((), (), s32[]{:S(2)}) async-start(), calls=%async_computation.3 | async-start | bytes 35651584 | tf_op jit(solution)/shard_map/all_gather | solution.py:9
  6.5 2.9 copy-start.3
  9.4 1.3 copy-start.4
  9.4 583.2 %all-gather.6.cloned.1.call-start = ((), (), s32[]{:S(2)}) async-start(), calls=%async_computation.1 | async-start | bytes 2228224 | tf_op jit(solution)/shard_map/all_gather | solution.py:65
  10.6 600.3 %reduce-scatter.2.cloned.1.call-start = ((), (), s32[]{:S(2)}) async-start(), calls=%async_computation.2 | async-start | bytes 2228224 | tf_op jit(solution)/shard_map/reduce_scatter | solution.py:69
  406.5 52.3 %copy-start.2 = (bf16[1,1024,128]{2,1,0:T(8,128)(2,1)S(1)}, bf16[1,1024,128]{2,1,0:T(8,128)(2,1)}, u32[]{:S(2)}) copy-start(bf16[1,1024,128]{2,1,0:T(8,128)(2,1)} %param.11) | copy-start | bytes 786436
  477.8 55.0 %copy-start.5 = (bf16[1,256,32]{1,2,0:T(8,128)(2,1)S(1)}, bf16[1,256,32]{1,2,0:T(8,128)(2,1)}, u32[]{:S(2)}) copy-start(bf16[1,256,32]{1,2,0:T(8,128)(2,1)} %param.9) | copy-start | bytes 49156
  592.7 20.6 %copy-start.1 = (bf16[1,16,128,256]{3,2,1,0:T(8,128)(2,1)S(1)}, bf16[1,16,128,256]{3,2,1,0:T(8,128)(2,1)}, u32[]{:S(2)}) copy-start(bf16[1,16,128,256]{3,2,1,0:T(8,128)(2,1)} %param.8) | copy-start | bytes 3145732
Sparse Core Ops, SparseCore 0:
  9.8 373.7 all-gather.7
  385.4 37.1 all-gather.5
  548.6 60.4 reduce-scatter.1
where the time goes:
time: 627 us; the launch traced here: 620 us
  waiting for transfers between devices  332 us (53%)
  local copies, waits for them, and re-layouts  134 us (21%)
  other arithmetic  54.6 us (9%)
  matrix products  44.1 us (7%)
  blocking collectives  40.8 us (7%)
  between operations  13.2 us (2%)
    all_gather x1, waiting for transfers between devices, carried_in(): pieces = jax.tree.map(lambda part: lax.all_gather(part, axis), value)  332 us
    reshape x2, local copies, waits for them, and re-layouts, shards(): incoming_adjoint.reshape(incoming_adjoint.shape[0], incoming_adjoint.shap...  99.1 us
    select_n x15, other arithmetic, turn(): jnp.where(position < mine, new, old)  51.8 us
    all_gather x1, blocking collectives, carried_in(): pieces = jax.tree.map(lambda part: lax.all_gather(part, axis), value)  40.8 us
    unnamed x14, local copies, waits for them, and re-layouts  23 us
    dot_general x1, matrix products, shards(): jnp.einsum('ixs,kx->isk', first_factor_adjoint, left_weight_matrix, prefe...  18.2 us
    dot_general x1, matrix products, shards(): jnp.einsum('mvpg,mpw->vgw', columns, first_factor_vectors, preferred_elem...  15.6 us
  transfers between devices with their start and end apart: 3, of which 1 were waited for; matrix products, arithmetic and copies ran while one was open for 37% of the time, Pallas kernels for 0%

commit v1 on v0

v1 whole, which is shorter than its diff:
```python
import jax
import jax.numpy as jnp
from jax import lax
from jax.experimental import pallas as pl
from jax.experimental.pallas import tpu as pltpu
from jax.sharding import PartitionSpec as P

MESH = pl.DeviceIdType.MESH
BF = jnp.bfloat16
F32 = jnp.float32
NSEC = 16
NRES = 16
ROWS = 16
SEQ = 128
CH = 256
W = 32
PC = 128
NX, NZ, NC = 4, 2, 2
JC = 128
YG = 4
YN = W // YG


def kernel(
    nrm_hbm, w1_hbm, w2_hbm, wout_hbm, pext_hbm, gain_hbm, out_hbm,
    nrm, w1, w2, wout, gain, gsend, gall,
    fr, bs, ph, wf, wp, lf, lt, rf, rall, osc, lacc, rg, c1, xs, xr, zs, zr, rgf, wt, outv,
    in_sem, gs_sem, gr_sem, fs_sem, fr_sem, bs_sem, br_sem, as_sem, ar_sem,
    cs_sem, cr_sem, xs_sem, xr_sem, zs_sem, zr_sem, out_sem,
):
    sec = lax.axis_index("section")
    res = lax.axis_index("res")
    mx, mz, mc = res // 4, lax.rem(res // 2, 2), lax.rem(res, 2)

    def at(x, z, c):
        return (sec, x * 4 + z * 2 + c)

    other_core = at(mx, mz, 1 - mc)
    other_z = at(mx, 1 - mz, mc)

    def x_peer(d):
        x = lax.rem(mx + d, NX)
        return x, at(x, mz, mc)

    loads = [
        pltpu.make_async_copy(src, dst, in_sem.at[n])
        for n, (src, dst) in enumerate(
            [(gain_hbm, gain), (nrm_hbm, nrm), (w1_hbm, w1), (w2_hbm, w2), (wout_hbm, wout)]
        )
    ]
    for load in loads:
        load.start()

    barrier = pltpu.get_barrier_semaphore()

    def greet(d, _):
        pl.semaphore_signal(
            barrier, inc=1, device_id=(lax.rem(sec + d, NSEC), res), device_id_type=MESH
        )
        return 0

    lax.fori_loop(1, NSEC, greet, 0)
    pl.semaphore_signal(barrier, inc=1, device_id=other_core, device_id_type=MESH)
    pl.semaphore_signal(barrier, inc=1, device_id=other_z, device_id_type=MESH)
    for d in range(1, NX):
        pl.semaphore_signal(barrier, inc=1, device_id=x_peer(d)[1], device_id_type=MESH)
    loads[0].wait()
    gsend[...] = jnp.broadcast_to(gain[...], gsend.shape)
    gall[sec] = gsend[...]
    pl.semaphore_wait(barrier, NSEC - 1 + 2 + NX - 1)

    def fwd(c, d):
        peer = lax.rem(sec + d, NSEC)
        return pltpu.make_async_remote_copy(
            src_ref=pext_hbm.at[peer, :, c],
            dst_ref=fr.at[c, sec],
            send_sem=fs_sem.at[c, d],
            recv_sem=fr_sem.at[c, sec],
            device_id=(peer, res),
            device_id_type=MESH,
        )

    def gains(d):
        peer = lax.rem(sec + d, NSEC)
        return pltpu.make_async_remote_copy(
            src_ref=gsend,
            dst_ref=gall.at[sec],
            send_sem=gs_sem.at[d],
            recv_sem=gr_sem.at[sec],
            device_id=(peer, res),
            device_id_type=MESH,
        )

    def own(c):
        return pltpu.make_async_copy(pext_hbm.at[sec, :, c], fr.at[c, sec], fr_sem.at[c, sec])

    def each(body, low=1, high=NSEC):
        def step(d, _):
            body(d)
            return 0

        lax.fori_loop(low, high, step, 0)

    each(lambda d: fwd(0, d).start())
    own(0).start()
    each(lambda d: gains(d).start())
    each(lambda d: fwd(1, d).start())
    own(1).start()

    loads[1].wait()
    loads[2].wait()
    loads[3].wait()
    wt[...] = jnp.concatenate([w1[...].astype(F32), w2[...].astype(F32)], axis=1).T.astype(BF)

    def project(n, _):
        block = nrm[pl.ds(n * 2, 2)].reshape(2 * SEQ, CH)
        both = lax.dot_general(
            wt[...], block, (((1,), (1,)), ((), ())), preferred_element_type=F32
        )
        for t in range(2):
            rows = pl.multiple_of((n * 2 + t) * W, W)
            lf[pl.ds(rows, W), :] = both[:W, t * SEQ : (t + 1) * SEQ]
            rf[pl.ds(rows, W), :] = both[W:, t * SEQ : (t + 1) * SEQ]
        return 0

    lax.fori_loop(0, ROWS // 2, project, 0)
    for y in range(W):
        rall[mx, mz, mc, y] = rf[pl.ds(y, ROWS, stride=W), :].astype(BF)

    def share(n, x, z, c, to):
        return pltpu.make_async_remote_copy(
            src_ref=rall.at[x, z, c],
            dst_ref=rall.at[x, z, c],
            send_sem=as_sem.at[n],
            recv_sem=ar_sem.at[x, z, c],
            device_id=to,
            device_id_type=MESH,
        )

    def arrived(x, z, c):
        pltpu.make_async_copy(rall.at[x, z, c], rall.at[x, z, c], ar_sem.at[x, z, c]).wait()

    shares = [share(0, mx, mz, mc, other_z)]
    shares += [share(d, mx, mz, mc, x_peer(d)[1]) for d in range(1, NX)]
    shares += [share(4, mx, mz, mc, other_core)]
    for copy in shares:
        copy.start()

    for n in range(4):
        lt[:, n * 128 : (n + 1) * 128] = lf[n * 128 : (n + 1) * 128, :].T.astype(BF)
    loads[4].wait()
    wf[...] = wout[...].astype(F32)
    for y in range(W):
        wp[y * W : (y + 1) * W, :] = wf[pl.ds(y, W, stride=W), :].astype(BF)
    lacc[...] = jnp.zeros_like(lacc)

    arrived(mx, 1 - mz, mc)
    more = [share(4 + d, mx, 1 - mz, mc, x_peer(d)[1]) for d in range(1, NX)]
    more += [share(8, mx, 1 - mz, mc, other_core)]
    for copy in more:
        copy.start()
    shares += more
    for d in range(1, NX):
        x = x_peer(d)[0]
        for z in (0, 1):
            arrived(x, z, mc)
            copy = share(7 + 2 * d + z, x, z, mc, other_core)
            copy.start()
            shares.append(copy)

    def back(c, d):
        peer = lax.rem(sec + d, NSEC)
        return pltpu.make_async_remote_copy(
            src_ref=bs.at[c, peer],
            dst_ref=ph.at[c, sec],
            send_sem=bs_sem.at[c, d],
            recv_sem=br_sem.at[c, sec],
            device_id=(peer, res),
            device_id_type=MESH,
        )

    def gain_arrived(d):
        k = lax.rem(sec + d, NSEC)
        pltpu.make_async_copy(gall.at[k], gall.at[k], gr_sem.at[k]).wait()

    def scan(c):
        if c == 0:
            each(gain_arrived)
        each(lambda k: pltpu.make_async_copy(fr.at[c, k], fr.at[c, k], fr_sem.at[c, k]).wait(), 0)

        def block(n, _):
            total = None
            for k in range(NSEC - 1, -1, -1):
                grad = fr[c, k, n].astype(F32)
                total = grad if total is None else grad + gall[k + 1, 0:1, :] * total
                bs[c, k, n] = total.astype(BF)
            return 0

        lax.fori_loop(0, NX, block, 0)
        pltpu.make_async_copy(bs.at[c, sec], ph.at[c, sec], br_sem.at[c, sec]).start()
        each(lambda d: back(c, d).start())

    def chunk(c):
        each(lambda k: pltpu.make_async_copy(ph.at[c, k], ph.at[c, k], br_sem.at[c, k]).wait(), 0)

        def outer(n, _):
            pair = ph[c, pl.ds(n * 2, 2)].reshape(2 * JC, PC)
            grad = lax.dot_general(
                wp[...], pair, (((1,), (1,)), ((), ())), preferred_element_type=F32
            ).astype(BF)
            for t in range(2):
                osc[n * 2 + t] = grad[:, t * JC : (t + 1) * JC].reshape(W, W, JC)
            return 0

        lax.fori_loop(0, ROWS // 2, outer, 0)

        def two(y):
            return jnp.concatenate(
                [osc[:, y + t].reshape(ROWS * W, JC) for t in range(2)], axis=1
            )

        def core_copy(g):
            ys = pl.ds(g * YN, YN)
            return pltpu.make_async_remote_copy(
                src_ref=rg.at[c, 1 - mc, :, ys],
                dst_ref=c1.at[c, :, ys],
                send_sem=cs_sem.at[c, g],
                recv_sem=cr_sem.at[c, g],
                device_id=other_core,
                device_id_type=MESH,
            )

        for g in range(YG):

            def right(n, _):
                y = g * YN + n * 2
                grad = jnp.dot(lt[...], two(y), preferred_element_type=F32)
                for t in range(2):
                    turned = grad[:, t * JC : (t + 1) * JC].T.astype(BF)
                    turned = turned.reshape(NX, NC, ROWS, SEQ)
                    for core in range(NC):
                        rg[c, core, :, y + t] = turned[:, core]
                return 0

            lax.fori_loop(0, YN // 2, right, 0)
            core_copy(g).start()

        def x_copy(g, d):
            ys = pl.ds(g * YN, YN)
            x, peer = x_peer(d)
            return pltpu.make_async_remote_copy(
                src_ref=xs.at[c, x, ys],
                dst_ref=xr.at[c, mx, ys],
                send_sem=xs_sem.at[c, g, d],
                recv_sem=xr_sem.at[c, g, mx],
                device_id=peer,
                device_id_type=MESH,
            )

        for g in range(YG):
            core_copy(g).wait_recv()

            def add_core(n, _):
                y = g * YN + n
                xs[c, :, y] = (
                    rg[c, mc, :, y].astype(F32) + c1[c, :, y].astype(F32)
                ).astype(BF)
                return 0

            lax.fori_loop(0, YN, add_core, 0)
            for d in range(1, NX):
                x_copy(g, d).start()

        def left(n, _):
            ys = n * 8
            terms = jnp.concatenate(
                [osc[:, ys + t].reshape(ROWS * W, JC) for t in range(8)], axis=1
            )
            vectors = jnp.concatenate(
                [rall[:, c, :, ys + t].reshape(JC, SEQ) for t in range(8)], axis=0
            )
            lacc[...] += jnp.dot(terms, vectors, preferred_element_type=F32)
            return 0

        if c == 0:
            for x in range(NX):
                for z in range(NZ):
                    arrived(x, z, 1 - mc)
        lax.fori_loop(0, W // 8, left, 0)

        def z_copy(g):
            ys = pl.ds(g * YN, YN)
            return pltpu.make_async_remote_copy(
                src_ref=zs.at[c, ys],
                dst_ref=zr.at[c, ys],
                send_sem=zs_sem.at[c, g],
                recv_sem=zr_sem.at[c, g],
                device_id=other_z,
                device_id_type=MESH,
            )

        for g in range(YG):
            for d in range(1, NX):
                x = x_peer(d)[0]
                part = xr.at[c, x, pl.ds(g * YN, YN)]
                pltpu.make_async_copy(part, part, xr_sem.at[c, g, x]).wait()

            def add_x(n, _):
                y = g * YN + n
                total = xs[c, mx, y].astype(F32)
                for d in range(1, NX):
                    total += xr[c, x_peer(d)[0], y].astype(F32)
                zs[c, y] = total.astype(BF)
                return 0

            lax.fori_loop(0, YN, add_x, 0)

            @pl.when(mz != c)
            def _():
                z_copy(g).start()

        @pl.when(mz == c)
        def _():
            for g in range(YG):
                z_copy(g).wait_recv()

                def add_z(n, _):
                    y = g * YN + n
                    rows = pl.multiple_of(y * ROWS, ROWS)
                    rgf[pl.ds(rows, ROWS), :] = zs[c, y].astype(F32) + zr[c, y].astype(F32)
                    return 0

                lax.fori_loop(0, YN, add_z, 0)

        def finish():
            for g in range(YG):
                core_copy(g).wait_send()
                for d in range(1, NX):
                    x_copy(g, d).wait_send()

            @pl.when(mz != c)
            def _():
                for g in range(YG):
                    z_copy(g).wait_send()

        return finish

    scan(0)
    scan(1)
    end0 = chunk(0)
    end1 = chunk(1)

    for i in range(ROWS):
        both = jnp.concatenate(
            [lacc[i * W : (i + 1) * W, :], rgf[pl.ds(i, W, stride=ROWS), :]], axis=0
        )
        both = (both * (1.0 / SEQ)).astype(BF)
        outv[i] = lax.dot_general(
            both, wt[...], (((0,), (0,)), ((), ())), preferred_element_type=F32
        ).astype(BF)
    done = pltpu.make_async_copy(outv, out_hbm, out_sem)
    done.start()

    for c in range(2):
        each(lambda d: fwd(c, d).wait_send())
        each(lambda d: back(c, d).wait_send())
    each(lambda d: gains(d).wait_send())
    for copy in shares:
        copy.wait_send()
    end0()
    end1()
    done.wait()


def shards(nrm, w1, w2, wout, pext, gain):
    anyspace = pl.BlockSpec(memory_space=pl.ANY)
    vm = pltpu.VMEM
    dma = pltpu.SemaphoreType.DMA
    out = pl.pallas_call(
        kernel,
        out_shape=jax.ShapeDtypeStruct((ROWS, SEQ, CH), BF),
        in_specs=[anyspace] * 6,
        out_specs=anyspace,
        scratch_shapes=[
            vm((ROWS, SEQ, CH), BF),
            vm((CH, W), BF),
            vm((CH, W), BF),
            vm((W * W, PC), BF),
            vm((1, PC), F32),
            vm((8, PC), F32),
            vm((NSEC, 8, PC), F32),
            vm((2, NSEC, NX, JC // NX, PC), BF),
            vm((2, NSEC, NX, JC // NX, PC), BF),
            vm((2, NSEC, NX, JC // NX, PC), BF),
            vm((W * W, PC), F32),
            vm((W * W, PC), BF),
            vm((ROWS * W, SEQ), F32),
            vm((SEQ, ROWS * W), BF),
            vm((ROWS * W, SEQ), F32),
            vm((NX, NZ, NC, W, ROWS, SEQ), BF),
            vm((ROWS, W, W, JC), BF),
            vm((ROWS * W, SEQ), F32),
            vm((2, NC, NX, W, ROWS, SEQ), BF),
            vm((2, NX, W, ROWS, SEQ), BF),
            vm((2, NX, W, ROWS, SEQ), BF),
            vm((2, NX, W, ROWS, SEQ), BF),
            vm((2, W, ROWS, SEQ), BF),
            vm((2, W, ROWS, SEQ), BF),
            vm((W * ROWS, SEQ), F32),
            vm((2 * W, CH), BF),
            vm((ROWS, SEQ, CH), BF),
            dma((5,)),
            dma((NSEC,)),
            dma((NSEC,)),
            dma((2, NSEC)),
            dma((2, NSEC)),
            dma((2, NSEC)),
            dma((2, NSEC)),
            dma((16,)),
            dma((NX, NZ, NC)),
            dma((2, YG)),
            dma((2, YG)),
            dma((2, YG, NX)),
            dma((2, YG, NX)),
            dma((2, YG)),
            dma((2, YG)),
            dma,
        ],
        compiler_params=pltpu.CompilerParams(
            collective_id=0, has_side_effects=True, vmem_limit_bytes=56 << 20
        ),
        cost_estimate=pl.CostEstimate(
            flops=3_400_000_000, bytes_accessed=4 << 20, transcendentals=0
        ),
        name="fused",
    )(
        nrm[0],
        w1[0],
        w2[0],
        wout[0],
        pext[0].reshape(ROWS, NX, NZ, JC // NX, PC),
        gain,
    )
    return out[None]


def solution(mesh):
    in_specs = (
        P("section", "res", None, None),
        P("section", None, None),
        P("section", None, None),
        P("section", None, None),
        P("section", "res", None, None),
        P("section", None),
    )
    out_specs = P("section", "res", None, None)
    return jax.shard_map(shards, mesh=mesh, in_specs=in_specs, out_specs=out_specs, check_vma=False)
```

time: 627 us -> 110 us (0.18)
  the two profiles are of different devices: /device:TPU:33 before, /device:TPU:32 now
where the time goes in v1:
time: 110 us
  Pallas kernels  105 us (95%)
  local copies, waits for them, and re-layouts  4.49 us (4%)
    pallas_call x1, Pallas kernels, shards(): pl.pallas_call(kernel, out_shape=jax.ShapeDtypeStruct((ROWS, SEQ, CH), BF...  105 us
    unnamed x5, local copies, waits for them, and re-layouts  4.49 us

profile of v1, /device:TPU:32, one launch (start us, length us, event | category | flops | bytes accessed | tf_op | source)
XLA Modules:
  0.0 109.9 jit_solution(10608119173556735763)
XLA Ops:
  0.0 0.0 copy-start
  0.0 1.5 %copy.7 = bf16[1,256,32]{2,1,0:T(8,128)(2,1)} copy(bf16[1,256,32]{1,2,0:T(8,128)(2,1)} %param.7) | data formatting | bytes 32768 | tf_op args[1]
  1.5 0.0 copy-done
  1.5 0.7 copy.8
  2.2 105.4 %fused.1 = bf16[16,128,256]{2,1,0:T(8,128)(2,1)} custom-call(bf16[16,128,256]{2,1,0:T(8,128)(2,1)} %bitcast.9, bf16[256,32]{1,0:T(8,128)(2,1)} %bitcast.7, bf16[256,32]{1,0:T(8,128)(2,1)} %bitcast.8, bf16[1024,128]{1,0:T(8,128)(2,1)} %bitcast.11, bf16[16,4,2,32,128]{4,3,2,1,0:T(8,128)(2,1)} %bitcast.10, f32[1,128]{1,0:T(1,128)} %gain_hbm.1), custom_call_target="tpu_custom_call" | custom-call | flops 3400000000 | bytes 4194304 | tf_op jit(solution)/shard_map/fused/pallas_call | solution.py:379
  107.6 2.3 %copy.10 = bf16[1,16,128,256]{3,2,1,0:T(8,128)(2,1)} copy(bf16[1,16,128,256]{3,2,1,0:T(8,128)(2,1)} %bitcast.6) | data formatting | bytes 2097152
Async XLA Ops:
  0.0 1.5 %copy-start = (bf16[1,256,32]{1,2,0:T(8,128)(2,1)S(1)}, bf16[1,256,32]{1,2,0:T(8,128)(2,1)}, u32[]{:S(2)}) copy-start(bf16[1,256,32]{1,2,0:T(8,128)(2,1)} %param.8) | copy-start | bytes 49156

commit v2 on v1

v2 whole, which is shorter than its diff:
```python
import jax
import jax.numpy as jnp
from jax import lax
from jax.experimental import pallas as pl
from jax.experimental.pallas import tpu as pltpu
from jax.sharding import PartitionSpec as P

MESH = pl.DeviceIdType.MESH
BF = jnp.bfloat16
F32 = jnp.float32
NSEC = 16
NRES = 16
ROWS = 16
SEQ = 128
CH = 256
W = 32
PC = 128
NX, NZ, NC = 4, 2, 2
NQ = NZ * NC
JC = NX * ROWS
YP = W // 2
YG = 2
YN = W // YG


def kernel(
    nrm_hbm, w1_hbm, w2_hbm, wout_hbm, pext_hbm, gain_hbm, out_hbm,
    nrm, w1, w2, wout, gain, gsend, gall,
    fr, bs, ph, wf, wp, lf, lt, rf, rall, osc, lacc, rg, c1, xs, xr, zs, zr, rgf, wt, outv,
    in_sem, gs_sem, gr_sem, fs_sem, fr_sem, bs_sem, br_sem, as_sem, ar_sem,
    cs_sem, cr_sem, xs_sem, xr_sem, zs_sem, zr_sem, out_sem,
):
    sec = lax.axis_index("section")
    res = lax.axis_index("res")
    mx, mz, mc = res // 4, lax.rem(res // 2, 2), lax.rem(res, 2)

    def at(x, z, c):
        return (sec, x * 4 + z * 2 + c)

    other_core = at(mx, mz, 1 - mc)
    other_z = at(mx, 1 - mz, mc)

    def x_peer(d):
        x = lax.rem(mx + d, NX)
        return x, at(x, mz, mc)

    loads = [
        pltpu.make_async_copy(src, dst, in_sem.at[n])
        for n, (src, dst) in enumerate(
            [(gain_hbm, gain), (nrm_hbm, nrm), (w1_hbm, w1), (w2_hbm, w2), (wout_hbm, wout)]
        )
    ]
    for load in loads:
        load.start()

    barrier = pltpu.get_barrier_semaphore()

    def greet(d, _):
        pl.semaphore_signal(
            barrier, inc=1, device_id=(lax.rem(sec + d, NSEC), res), device_id_type=MESH
        )
        return 0

    lax.fori_loop(1, NSEC, greet, 0)
    pl.semaphore_signal(barrier, inc=1, device_id=other_core, device_id_type=MESH)
    pl.semaphore_signal(barrier, inc=1, device_id=other_z, device_id_type=MESH)
    for d in range(1, NX):
        pl.semaphore_signal(barrier, inc=1, device_id=x_peer(d)[1], device_id_type=MESH)
    loads[0].wait()
    gsend[...] = jnp.broadcast_to(gain[...], gsend.shape)
    gall[sec] = gsend[...]
    pl.semaphore_wait(barrier, NSEC - 1 + 2 + NX - 1)

    def fwd(c, d):
        peer = lax.rem(sec + d, NSEC)
        return pltpu.make_async_remote_copy(
            src_ref=pext_hbm.at[peer, :, c],
            dst_ref=fr.at[c, sec],
            send_sem=fs_sem.at[c, d],
            recv_sem=fr_sem.at[c, sec],
            device_id=(peer, res),
            device_id_type=MESH,
        )

    def gains(d):
        peer = lax.rem(sec + d, NSEC)
        return pltpu.make_async_remote_copy(
            src_ref=gsend,
            dst_ref=gall.at[sec],
            send_sem=gs_sem.at[d],
            recv_sem=gr_sem.at[sec],
            device_id=(peer, res),
            device_id_type=MESH,
        )

    def each(body, low=1, high=NSEC):
        def step(d, _):
            body(d)
            return 0

        lax.fori_loop(low, high, step, 0)

    def send_fwd(c):
        each(lambda d: fwd(c, d).start())
        pltpu.make_async_copy(pext_hbm.at[sec, :, c], fr.at[c, sec], fr_sem.at[c, sec]).start()

    send_fwd(0)
    each(lambda d: gains(d).start())
    send_fwd(1)

    loads[1].wait()
    loads[2].wait()
    loads[3].wait()
    wt[:W] = w1[...]
    wt[W:] = w2[...]

    def project(n, _):
        block = nrm[pl.ds(n * 2, 2)].reshape(2 * SEQ, CH)
        both = lax.dot_general(
            wt[...], block, (((1,), (1,)), ((), ())), preferred_element_type=F32
        )
        for t in range(2):
            rows = pl.multiple_of((n * 2 + t) * W, W)
            lf[pl.ds(rows, W), :] = both[:W, t * SEQ : (t + 1) * SEQ]
            rf[pl.ds(rows, W), :] = both[W:, t * SEQ : (t + 1) * SEQ]
        return 0

    lax.fori_loop(0, ROWS // 2, project, 0)
    for y in range(W):
        rall[mx, mz, mc, y] = rf[pl.ds(y, ROWS, stride=W), :].astype(BF)

    def share(n, x, z, c, to):
        return pltpu.make_async_remote_copy(
            src_ref=rall.at[x, z, c],
            dst_ref=rall.at[x, z, c],
            send_sem=as_sem.at[n],
            recv_sem=ar_sem.at[x, z, c],
            device_id=to,
            device_id_type=MESH,
        )

    def arrived(x, z, c):
        pltpu.make_async_copy(rall.at[x, z, c], rall.at[x, z, c], ar_sem.at[x, z, c]).wait()

    shares = []

    def pass_on(copies):
        for copy in copies:
            copy.start()
        shares.extend(copies)

    pass_on(
        [share(0, mx, mz, mc, other_z)]
        + [share(d, mx, mz, mc, x_peer(d)[1]) for d in range(1, NX)]
        + [share(4, mx, mz, mc, other_core)]
    )
    send_fwd(2)
    send_fwd(3)

    for n in range(4):
        lt[:, n * 128 : (n + 1) * 128] = lf[n * 128 : (n + 1) * 128, :].T.astype(BF)
    loads[4].wait()
    wf[...] = wout[...].astype(F32)
    for y in range(W):
        wp[(y // 2) * W : (y // 2 + 1) * W, (y % 2) * PC : (y % 2 + 1) * PC] = wf[
            pl.ds(y, W, stride=W), :
        ].astype(BF)
    lacc[...] = jnp.zeros_like(lacc)

    def pass_z():
        arrived(mx, 1 - mz, mc)
        pass_on(
            [share(4 + d, mx, 1 - mz, mc, x_peer(d)[1]) for d in range(1, NX)]
            + [share(8, mx, 1 - mz, mc, other_core)]
        )

    def pass_x(n):
        for d in range(1, NX):
            x = x_peer(d)[0]
            z = mz if n == 0 else 1 - mz
            arrived(x, z, mc)
            pass_on([share(7 + 2 * d + n, x, z, mc, other_core)])

    def back(c, d):
        peer = lax.rem(sec + d, NSEC)
        return pltpu.make_async_remote_copy(
            src_ref=bs.at[c, peer],
            dst_ref=ph.at[c, sec],
            send_sem=bs_sem.at[c, d],
            recv_sem=br_sem.at[c, sec],
            device_id=(peer, res),
            device_id_type=MESH,
        )

    def gain_arrived(d):
        k = lax.rem(sec + d, NSEC)
        pltpu.make_async_copy(gall.at[k], gall.at[k], gr_sem.at[k]).wait()

    def scan(c):
        if c == 0:
            each(gain_arrived)
        each(lambda k: pltpu.make_async_copy(fr.at[c, k], fr.at[c, k], fr_sem.at[c, k]).wait(), 0)
        total = None
        for k in range(NSEC - 1, -1, -1):
            grad = fr[c, k].reshape(JC, PC).astype(F32)
            total = grad if total is None else grad + gall[k + 1, 0:1, :] * total
            bs[c, k] = total.astype(BF).reshape(NX, ROWS, PC)
        pltpu.make_async_copy(bs.at[c, sec], ph.at[c, sec], br_sem.at[c, sec]).start()
        each(lambda d: back(c, d).start())

    def core_copy(c, g):
        ys = pl.ds(g * YN, YN)
        return pltpu.make_async_remote_copy(
            src_ref=rg.at[c, :, ys],
            dst_ref=c1.at[c // 2, :, ys],
            send_sem=cs_sem.at[c, g],
            recv_sem=cr_sem.at[c // 2, g],
            device_id=other_core,
            device_id_type=MESH,
        )

    def x_copy(c, g, d):
        ys = pl.ds(g * YN, YN)
        x, peer = x_peer(d)
        return pltpu.make_async_remote_copy(
            src_ref=xs.at[c // 2, x, ys],
            dst_ref=xr.at[c // 2, mx, ys],
            send_sem=xs_sem.at[c // 2, g, d],
            recv_sem=xr_sem.at[c // 2, g, mx],
            device_id=peer,
            device_id_type=MESH,
        )

    def z_copy(g):
        ys = pl.ds(g * YN, YN)
        return pltpu.make_async_remote_copy(
            src_ref=zs.at[1 - mz, ys],
            dst_ref=zr.at[ys],
            send_sem=zs_sem.at[g],
            recv_sem=zr_sem.at[g],
            device_id=other_z,
            device_id_type=MESH,
        )

    def products(c):
        def outer(n, _):
            wide = []
            for t in range(2):
                i = lax.rem(sec - n * 2 - t + NSEC, NSEC)
                pltpu.make_async_copy(ph.at[c, i], ph.at[c, i], br_sem.at[c, i]).wait()
                pair = ph[c, i].reshape(JC, PC)
                none = jnp.zeros_like(pair)
                wide += [
                    jnp.concatenate([pair, none], axis=1),
                    jnp.concatenate([none, pair], axis=1),
                ]
            grad = lax.dot_general(
                wp[...],
                jnp.concatenate(wide, axis=0),
                (((1,), (1,)), ((), ())),
                preferred_element_type=F32,
            ).astype(BF)
            for t in range(2):
                i = lax.rem(sec - n * 2 - t + NSEC, NSEC)
                osc[i] = grad[:, t * 2 * JC : (t + 1) * 2 * JC].reshape(YP, W, 2 * JC)
            return 0

        lax.fori_loop(0, ROWS // 2, outer, 0)

        for g in range(YG):

            def right(n, _):
                yp = g * (YN // 2) + n * 2
                both = jnp.concatenate(
                    [osc[:, yp + t].reshape(ROWS * W, 2 * JC) for t in range(2)], axis=1
                )
                grad = jnp.dot(lt[...], both, preferred_element_type=F32)
                for t in range(2):
                    turned = grad[:, t * 2 * JC : (t + 1) * 2 * JC].T.astype(BF)
                    turned = turned.reshape(2, NX, ROWS, SEQ)
                    for u in range(2):
                        rg[c, :, (yp + t) * 2 + u] = turned[u]
                return 0

            lax.fori_loop(0, YN // 4, right, 0)

            @pl.when(mc != c % 2)
            def _():
                core_copy(c, g).start()

        def left(n, _):
            terms = jnp.concatenate(
                [osc[:, n * 8 + t].reshape(ROWS * W, 2 * JC) for t in range(8)], axis=1
            )
            vectors = jnp.concatenate(
                [rall[:, c // 2, c % 2, n * 16 + t].reshape(JC, SEQ) for t in range(16)], axis=0
            )
            lacc[...] += jnp.dot(terms, vectors, preferred_element_type=F32)
            return 0

        lax.fori_loop(0, YP // 8, left, 0)

    def over_cores(c):
        @pl.when(mc == c % 2)
        def _():
            for g in range(YG):
                core_copy(c, g).wait_recv()

                def add_core(n, _):
                    y = g * YN + n
                    xs[c // 2, :, y] = (
                        rg[c, :, y].astype(F32) + c1[c // 2, :, y].astype(F32)
                    ).astype(BF)
                    return 0

                lax.fori_loop(0, YN, add_core, 0)
                for d in range(1, NX):
                    x_copy(c, g, d).start()

    def over_x(c):
        @pl.when(mc == c % 2)
        def _():
            for g in range(YG):
                for d in range(1, NX):
                    x = x_peer(d)[0]
                    part = xr.at[c // 2, x, pl.ds(g * YN, YN)]
                    pltpu.make_async_copy(part, part, xr_sem.at[c // 2, g, x]).wait()

                def add_x(n, _):
                    y = g * YN + n
                    total = xs[c // 2, mx, y].astype(F32)
                    for d in range(1, NX):
                        total += xr[c // 2, x_peer(d)[0], y].astype(F32)
                    zs[c // 2, y] = total.astype(BF)
                    return 0

                lax.fori_loop(0, YN, add_x, 0)

                @pl.when(mz != c // 2)
                def _():
                    z_copy(g).start()

    def over_z():
        for g in range(YG):
            z_copy(g).wait_recv()

            def add_z(n, _):
                y = g * YN + n
                rows = pl.multiple_of(y * ROWS, ROWS)
                rgf[pl.ds(rows, ROWS), :] = zs[mz, y].astype(F32) + zr[y].astype(F32)
                return 0

            lax.fori_loop(0, YN, add_z, 0)

    pass_z()
    scan(0)
    pass_x(0)
    scan(1)
    pass_x(1)
    scan(2)
    scan(3)
    for x in range(NX):
        for z in range(NZ):
            arrived(x, z, 1 - mc)
    for c in range(NQ):
        products(c)
        if c:
            over_x(c - 1)
        over_cores(c)
    over_x(NQ - 1)
    over_z()

    for i in range(ROWS):
        both = jnp.concatenate(
            [lacc[i * W : (i + 1) * W, :], rgf[pl.ds(i, W, stride=ROWS), :]], axis=0
        )
        both = (both * (1.0 / SEQ)).astype(BF)
        outv[i] = lax.dot_general(
            both, wt[...], (((0,), (0,)), ((), ())), preferred_element_type=F32
        ).astype(BF)
    done = pltpu.make_async_copy(outv, out_hbm, out_sem)
    done.start()

    for c in range(NQ):
        each(lambda d: fwd(c, d).wait_send())
        each(lambda d: back(c, d).wait_send())
    each(lambda d: gains(d).wait_send())
    for copy in shares:
        copy.wait_send()
    for c in range(NQ):
        for g in range(YG):

            @pl.when(mc != c % 2)
            def _():
                core_copy(c, g).wait_send()

            @pl.when(mc == c % 2)
            def _():
                for d in range(1, NX):
                    x_copy(c, g, d).wait_send()

    for g in range(YG):
        z_copy(g).wait_send()
    done.wait()


def shards(nrm, w1, w2, wout, pext, gain):
    anyspace = pl.BlockSpec(memory_space=pl.ANY)
    vm = pltpu.VMEM
    dma = pltpu.SemaphoreType.DMA
    out = pl.pallas_call(
        kernel,
        out_shape=jax.ShapeDtypeStruct((ROWS, SEQ, CH), BF),
        in_specs=[anyspace] * 6,
        out_specs=anyspace,
        scratch_shapes=[
            vm((ROWS, SEQ, CH), BF),
            vm((W, CH), BF),
            vm((W, CH), BF),
            vm((W * W, PC), BF),
            vm((1, PC), F32),
            vm((8, PC), F32),
            vm((NSEC, 8, PC), F32),
            vm((NQ, NSEC, NX, ROWS, PC), BF),
            vm((NQ, NSEC, NX, ROWS, PC), BF),
            vm((NQ, NSEC, NX, ROWS, PC), BF),
            vm((W * W, PC), F32),
            vm((YP * W, 2 * PC), BF),
            vm((ROWS * W, SEQ), F32),
            vm((SEQ, ROWS * W), BF),
            vm((ROWS * W, SEQ), F32),
            vm((NX, NZ, NC, W, ROWS, SEQ), BF),
            vm((ROWS, YP, W, 2 * JC), BF),
            vm((ROWS * W, SEQ), F32),
            vm((NQ, NX, W, ROWS, SEQ), BF),
            vm((2, NX, W, ROWS, SEQ), BF),
            vm((2, NX, W, ROWS, SEQ), BF),
            vm((2, NX, W, ROWS, SEQ), BF),
            vm((2, W, ROWS, SEQ), BF),
            vm((W, ROWS, SEQ), BF),
            vm((W * ROWS, SEQ), F32),
            vm((2 * W, CH), BF),
            vm((ROWS, SEQ, CH), BF),
            dma((5,)),
            dma((NSEC,)),
            dma((NSEC,)),
            dma((NQ, NSEC)),
            dma((NQ, NSEC)),
            dma((NQ, NSEC)),
            dma((NQ, NSEC)),
            dma((16,)),
            dma((NX, NZ, NC)),
            dma((NQ, YG)),
            dma((NZ, YG)),
            dma((NZ, YG, NX)),
            dma((NZ, YG, NX)),
            dma((YG,)),
            dma((YG,)),
            dma,
        ],
        compiler_params=pltpu.CompilerParams(
            collective_id=0, has_side_effects=True, vmem_limit_bytes=56 << 20
        ),
        cost_estimate=pl.CostEstimate(
            flops=3_400_000_000, bytes_accessed=4 << 20, transcendentals=0
        ),
        name="fused",
    )(
        nrm[0],
        jnp.swapaxes(w1[0], 0, 1),
        jnp.swapaxes(w2[0], 0, 1),
        wout[0],
        pext[0].reshape(ROWS, NX, NQ, ROWS, PC),
        gain,
    )
    return out[None]


def solution(mesh):
    in_specs = (
        P("section", "res", None, None),
        P("section", None, None),
        P("section", None, None),
        P("section", None, None),
        P("section", "res", None, None),
        P("section", None),
    )
    out_specs = P("section", "res", None, None)
    return jax.shard_map(shards, mesh=mesh, in_specs=in_specs, out_specs=out_specs, check_vma=False)
```

time: 110 us -> 90.2 us (0.82)
  the two profiles are of different devices: /device:TPU:32 before, /device:TPU:33 now
where the time goes in v2:
time: 90.2 us; the launch traced here: 89.9 us
  Pallas kernels  87.6 us (97%)
  local copies, waits for them, and re-layouts  2.29 us (3%)
    pallas_call x1, Pallas kernels, shards(): pl.pallas_call(kernel, out_shape=jax.ShapeDtypeStruct((ROWS, SEQ, CH), BF...  87.6 us
    unnamed x1, local copies, waits for them, and re-layouts  2.29 us

profile of v2, /device:TPU:33, one launch (start us, length us, event | category | flops | bytes accessed | tf_op | source)
XLA Modules:
  0.0 89.9 jit_solution(3333158087166978400)
XLA Ops:
  0.0 87.6 %fused.1 = bf16[16,128,256]{2,1,0:T(8,128)(2,1)} custom-call(bf16[16,128,256]{2,1,0:T(8,128)(2,1)} %bitcast.11, bf16[32,256]{1,0:T(8,128)(2,1)} %bitcast.14, bf16[32,256]{1,0:T(8,128)(2,1)} %bitcast.15, bf16[1024,128]{1,0:T(8,128)(2,1)} %bitcast.13, bf16[16,4,4,16,128]{4,3,2,1,0:T(8,128)(2,1)} %bitcast.12, f32[1,128]{1,0:T(1,128)} %gain_hbm.1), custom_call_target="tpu_custom_call" | custom-call | flops 3400000000 | bytes 4194304 | tf_op jit(solution)/shard_map/fused/pallas_call | solution.py:411
  87.6 2.3 %copy.8 = bf16[1,16,128,256]{3,2,1,0:T(8,128)(2,1)} copy(bf16[1,16,128,256]{3,2,1,0:T(8,128)(2,1)} %bitcast.10) | data formatting | bytes 2097152

commit v3 on v2

--- a/solution.py
+++ b/solution.py
@@ -19,14 +19,15 @@
 NQ = NZ * NC
 JC = NX * ROWS
 YP = W // 2
-YG = 2
+YG = 4
 YN = W // YG
+STEP = 8
 
 
 def kernel(
-    nrm_hbm, w1_hbm, w2_hbm, wout_hbm, pext_hbm, gain_hbm, out_hbm,
+    nrm_hbm, w1_hbm, w2_hbm, wout_hbm, pext_hbm, gain_hbm, lr_hbm,
     nrm, w1, w2, wout, gain, gsend, gall,
-    fr, bs, ph, wf, wp, lf, lt, rf, rall, osc, lacc, rg, c1, xs, xr, zs, zr, rgf, wt, outv,
+    fr, bs, ph, wf, wp, lf, lt, rf, rall, osc, lacc, rg, c1, xs, xr, zs, zr, rgf, wt, lrv,
     in_sem, gs_sem, gr_sem, fs_sem, fr_sem, bs_sem, br_sem, as_sem, ar_sem,
     cs_sem, cr_sem, xs_sem, xr_sem, zs_sem, zr_sem, out_sem,
 ):
@@ -244,53 +245,56 @@
 
     def products(c):
         def outer(n, _):
-            wide = []
-            for t in range(2):
-                i = lax.rem(sec - n * 2 - t + NSEC, NSEC)
+            rows = [lax.rem(sec - n * 4 - t + NSEC, NSEC) for t in range(4)]
+            for i in rows:
                 pltpu.make_async_copy(ph.at[c, i], ph.at[c, i], br_sem.at[c, i]).wait()
-                pair = ph[c, i].reshape(JC, PC)
-                none = jnp.zeros_like(pair)
-                wide += [
-                    jnp.concatenate([pair, none], axis=1),
-                    jnp.concatenate([none, pair], axis=1),
-                ]
-            grad = lax.dot_general(
-                wp[...],
-                jnp.concatenate(wide, axis=0),
-                (((1,), (1,)), ((), ())),
-                preferred_element_type=F32,
-            ).astype(BF)
-            for t in range(2):
-                i = lax.rem(sec - n * 2 - t + NSEC, NSEC)
-                osc[i] = grad[:, t * 2 * JC : (t + 1) * 2 * JC].reshape(YP, W, 2 * JC)
+            for two in (rows[:2], rows[2:]):
+                wide = []
+                for i in two:
+                    pair = ph[c, i].reshape(JC, PC)
+                    none = jnp.zeros_like(pair)
+                    wide += [
+                        jnp.concatenate([pair, none], axis=1),
+                        jnp.concatenate([none, pair], axis=1),
+                    ]
+                grad = lax.dot_general(
+                    wp[...],
+                    jnp.concatenate(wide, axis=0),
+                    (((1,), (1,)), ((), ())),
+                    preferred_element_type=F32,
+                ).astype(BF)
+                for t, i in enumerate(two):
+                    osc[c, i] = grad[:, t * 2 * JC : (t + 1) * 2 * JC].reshape(YP, W, 2 * JC)
             return 0
 
-        lax.fori_loop(0, ROWS // 2, outer, 0)
+        lax.fori_loop(0, ROWS // 4, outer, 0)
 
         for g in range(YG):
 
             def right(n, _):
-                yp = g * (YN // 2) + n * 2
-                both = jnp.concatenate(
-                    [osc[:, yp + t].reshape(ROWS * W, 2 * JC) for t in range(2)], axis=1
-                )
-                grad = jnp.dot(lt[...], both, preferred_element_type=F32)
-                for t in range(2):
-                    turned = grad[:, t * 2 * JC : (t + 1) * 2 * JC].T.astype(BF)
-                    turned = turned.reshape(2, NX, ROWS, SEQ)
-                    for u in range(2):
-                        rg[c, :, (yp + t) * 2 + u] = turned[u]
+                for h in range(2):
+                    yp = g * (YN // 2) + n * 4 + h * 2
+                    both = jnp.concatenate(
+                        [osc[c, :, yp + t].reshape(ROWS * W, 2 * JC) for t in range(2)], axis=1
+                    )
+                    grad = jnp.dot(lt[...], both, preferred_element_type=F32)
+                    for t in range(2):
+                        turned = grad[:, t * 2 * JC : (t + 1) * 2 * JC].T.astype(BF)
+                        turned = turned.reshape(2, NX, ROWS, SEQ)
+                        for u in range(2):
+                            rg[c, :, (yp + t) * 2 + u] = turned[u]
                 return 0
 
-            lax.fori_loop(0, YN // 4, right, 0)
+            lax.fori_loop(0, YN // 8, right, 0)
 
             @pl.when(mc != c % 2)
             def _():
                 core_copy(c, g).start()
 
+    def left_products(c):
         def left(n, _):
             terms = jnp.concatenate(
-                [osc[:, n * 8 + t].reshape(ROWS * W, 2 * JC) for t in range(8)], axis=1
+                [osc[c, :, n * 8 + t].reshape(ROWS * W, 2 * JC) for t in range(8)], axis=1
             )
             vectors = jnp.concatenate(
                 [rall[:, c // 2, c % 2, n * 16 + t].reshape(JC, SEQ) for t in range(16)], axis=0
@@ -352,33 +356,32 @@
 
             lax.fori_loop(0, YN, add_z, 0)
 
+    scan(0)
     pass_z()
-    scan(0)
+    scan(1)
+    scan(2)
     pass_x(0)
-    scan(1)
+    scan(3)
     pass_x(1)
-    scan(2)
-    scan(3)
-    for x in range(NX):
-        for z in range(NZ):
-            arrived(x, z, 1 - mc)
     for c in range(NQ):
         products(c)
+        if c == 1:
+            for x in range(NX):
+                for z in range(NZ):
+                    arrived(x, z, 1 - mc)
         if c:
+            left_products(c - 1)
             over_x(c - 1)
         over_cores(c)
+    left_products(NQ - 1)
+    for i in range(ROWS):
+        lrv[i, :W] = (lacc[i * W : (i + 1) * W, :] * (1.0 / SEQ)).astype(BF)
     over_x(NQ - 1)
     over_z()
 
     for i in range(ROWS):
-        both = jnp.concatenate(
-            [lacc[i * W : (i + 1) * W, :], rgf[pl.ds(i, W, stride=ROWS), :]], axis=0
-        )
-        both = (both * (1.0 / SEQ)).astype(BF)
-        outv[i] = lax.dot_general(
-            both, wt[...], (((0,), (0,)), ((), ())), preferred_element_type=F32
-        ).astype(BF)
-    done = pltpu.make_async_copy(outv, out_hbm, out_sem)
+        lrv[i, W:] = (rgf[pl.ds(i, W, stride=ROWS), :] * (1.0 / SEQ)).astype(BF)
+    done = pltpu.make_async_copy(lrv, lr_hbm, out_sem)
     done.start()
 
     for c in range(NQ):
@@ -404,13 +407,23 @@
     done.wait()
 
 
+def project_out(lr, w1, w2, out):
+    weights = jnp.concatenate([w1[...], w2[...]], axis=0)
+    for t in range(STEP):
+        out[t] = lax.dot_general(
+            lr[t], weights, (((0,), (0,)), ((), ())), preferred_element_type=F32
+        ).astype(BF)
+
+
 def shards(nrm, w1, w2, wout, pext, gain):
     anyspace = pl.BlockSpec(memory_space=pl.ANY)
     vm = pltpu.VMEM
     dma = pltpu.SemaphoreType.DMA
-    out = pl.pallas_call(
+    w1t = jnp.swapaxes(w1[0], 0, 1)
+    w2t = jnp.swapaxes(w2[0], 0, 1)
+    lr = pl.pallas_call(
         kernel,
-        out_shape=jax.ShapeDtypeStruct((ROWS, SEQ, CH), BF),
+        out_shape=jax.ShapeDtypeStruct((ROWS, 2 * W, SEQ), BF),
         in_specs=[anyspace] * 6,
         out_specs=anyspace,
         scratch_shapes=[
@@ -430,7 +443,7 @@
             vm((SEQ, ROWS * W), BF),
             vm((ROWS * W, SEQ), F32),
             vm((NX, NZ, NC, W, ROWS, SEQ), BF),
-            vm((ROWS, YP, W, 2 * JC), BF),
+            vm((NQ, ROWS, YP, W, 2 * JC), BF),
             vm((ROWS * W, SEQ), F32),
             vm((NQ, NX, W, ROWS, SEQ), BF),
             vm((2, NX, W, ROWS, SEQ), BF),
@@ -440,7 +453,7 @@
             vm((W, ROWS, SEQ), BF),
             vm((W * ROWS, SEQ), F32),
             vm((2 * W, CH), BF),
-            vm((ROWS, SEQ, CH), BF),
+            vm((ROWS, 2 * W, SEQ), BF),
             dma((5,)),
             dma((NSEC,)),
             dma((NSEC,)),
@@ -467,12 +480,24 @@
         name="fused",
     )(
         nrm[0],
-        jnp.swapaxes(w1[0], 0, 1),
-        jnp.swapaxes(w2[0], 0, 1),
+        w1t,
+        w2t,
         wout[0],
         pext[0].reshape(ROWS, NX, NQ, ROWS, PC),
         gain,
     )
+    out = pl.pallas_call(
+        project_out,
+        out_shape=jax.ShapeDtypeStruct((ROWS, SEQ, CH), BF),
+        grid=(ROWS // STEP,),
+        in_specs=[
+            pl.BlockSpec((STEP, 2 * W, SEQ), lambda n: (n, 0, 0)),
+            pl.BlockSpec((W, CH), lambda n: (0, 0)),
+            pl.BlockSpec((W, CH), lambda n: (0, 0)),
+        ],
+        out_specs=pl.BlockSpec((STEP, SEQ, CH), lambda n: (n, 0, 0)),
+        name="project_out",
+    )(lr, w1t, w2t)
     return out[None]
 
 

time: 90.2 us -> 85 us (0.942)
  Pallas kernels: 87.6 us -> 84.9 us
  local copies, waits for them, and re-layouts: 2.29 us -> 0 us
    pallas_call x1 -> x2, Pallas kernels: 87.6 us -> 84.9 us  [the longest x1 82.5 us: shards(): pl.pallas_call(kernel, out_shape=jax.ShapeDtypeStruct((ROWS, 2 * W, SEQ),...]
    unnamed x1 -> x0, local copies, waits for them, and re-layouts: 2.29 us -> none
where the time goes in v3:
time: 85 us; the launch traced here: 84.9 us
  Pallas kernels  84.9 us (100%)
    pallas_call x1, Pallas kernels, shards(): pl.pallas_call(kernel, out_shape=jax.ShapeDtypeStruct((ROWS, 2 * W, SEQ),...  82.5 us
    pallas_call x1, Pallas kernels, shards(): pl.pallas_call(project_out, out_shape=jax.ShapeDtypeStruct((ROWS, SEQ, CH...  2.39 us

profile of v3, /device:TPU:33, one launch (start us, length us, event | category | flops | bytes accessed | tf_op | source)
XLA Modules:
  0.0 84.9 jit_solution(7627015946021173502)
XLA Ops:
  0.0 82.5 %fused.1.lr = bf16[16,64,128]{2,1,0:T(8,128)(2,1)} custom-call(bf16[16,128,256]{2,1,0:T(8,128)(2,1)} %bitcast.14, bf16[32,256]{1,0:T(8,128)(2,1)} %bitcast.10, bf16[32,256]{1,0:T(8,128)(2,1)} %bitcast.12, bf16[1024,128]{1,0:T(8,128)(2,1)} %bitcast.16, bf16[16,4,4,16,128]{4,3,2,1,0:T(8,128)(2,1)} %bitcast.15, f32[1,128]{1,0:T(1,128)} %gain_hbm.1), custom_call_target="tpu_custom_call" | custom-call | flops 3400000000 | bytes 4194304 | tf_op jit(solution)/shard_map/fused/pallas_call | solution.py:424
  82.5 2.4 %project_out.1 = bf16[16,128,256]{2,1,0:T(8,128)(2,1)} custom-call(bf16[16,64,128]{2,1,0:T(8,128)(2,1)} %fused.1.lr, bf16[32,256]{1,0:T(8,128)(2,1)} %bitcast.11, bf16[32,256]{1,0:T(8,128)(2,1)} %bitcast.13), custom_call_target="tpu_custom_call" | custom-call | tf_op jit(solution)/shard_map/project_out/pallas_call | solution.py:489

commit v4 on v3

--- a/solution.py
+++ b/solution.py
@@ -108,6 +108,8 @@
     send_fwd(0)
     each(lambda d: gains(d).start())
     send_fwd(1)
+    send_fwd(2)
+    send_fwd(3)
 
     loads[1].wait()
     loads[2].wait()
@@ -155,8 +157,6 @@
         + [share(d, mx, mz, mc, x_peer(d)[1]) for d in range(1, NX)]
         + [share(4, mx, mz, mc, other_core)]
     )
-    send_fwd(2)
-    send_fwd(3)
 
     for n in range(4):
         lt[:, n * 128 : (n + 1) * 128] = lf[n * 128 : (n + 1) * 128, :].T.astype(BF)
@@ -356,26 +356,65 @@
 
             lax.fori_loop(0, YN, add_z, 0)
 
+    def sent_fwd():
+        for c in range(NQ):
+            each(lambda d: fwd(c, d).wait_send())
+        each(lambda d: gains(d).wait_send())
+
+    def sent_back():
+        for c in range(NQ):
+            each(lambda d: back(c, d).wait_send())
+        for copy in shares:
+            copy.wait_send()
+
+    def sent(c):
+        @pl.when(mc != c % 2)
+        def _():
+            for g in range(YG):
+                core_copy(c, g).wait_send()
+
+        @pl.when(mc == c % 2)
+        def _():
+            for g in range(YG):
+                for d in range(1, NX):
+                    x_copy(c, g, d).wait_send()
+
+    def sent_z():
+        for g in range(YG):
+            z_copy(g).wait_send()
+
     scan(0)
-    pass_z()
     scan(1)
     scan(2)
+    scan(3)
+    pass_z()
     pass_x(0)
-    scan(3)
+    products(0)
+    over_cores(0)
     pass_x(1)
-    for c in range(NQ):
-        products(c)
-        if c == 1:
-            for x in range(NX):
-                for z in range(NZ):
-                    arrived(x, z, 1 - mc)
-        if c:
-            left_products(c - 1)
-            over_x(c - 1)
-        over_cores(c)
-    left_products(NQ - 1)
+    products(1)
+    over_x(0)
+    over_cores(1)
+    products(2)
+    for x in range(NX):
+        for z in range(NZ):
+            arrived(x, z, 1 - mc)
+    left_products(0)
+    left_products(1)
+    over_x(1)
+    over_cores(2)
+    sent_fwd()
+    products(3)
+    over_x(2)
+    over_cores(3)
+    left_products(2)
+    left_products(3)
     for i in range(ROWS):
         lrv[i, :W] = (lacc[i * W : (i + 1) * W, :] * (1.0 / SEQ)).astype(BF)
+    sent(0)
+    sent(1)
+    sent(2)
+    sent_back()
     over_x(NQ - 1)
     over_z()
 
@@ -383,27 +422,9 @@
         lrv[i, W:] = (rgf[pl.ds(i, W, stride=ROWS), :] * (1.0 / SEQ)).astype(BF)
     done = pltpu.make_async_copy(lrv, lr_hbm, out_sem)
     done.start()
-
-    for c in range(NQ):
-        each(lambda d: fwd(c, d).wait_send())
-        each(lambda d: back(c, d).wait_send())
-    each(lambda d: gains(d).wait_send())
-    for copy in shares:
-        copy.wait_send()
-    for c in range(NQ):
-        for g in range(YG):
-
-            @pl.when(mc != c % 2)
-            def _():
-                core_copy(c, g).wait_send()
-
-            @pl.when(mc == c % 2)
-            def _():
-                for d in range(1, NX):
-                    x_copy(c, g, d).wait_send()
-
-    for g in range(YG):
-        z_copy(g).wait_send()
+    sent(3)
+    sent_z()
+
     done.wait()
 
 

time: 85 us -> 79.8 us (0.939)
  Pallas kernels: 84.9 us -> 79.6 us
    pallas_call x1, Pallas kernels: 82.5 us -> 77.3 us  [shards(): pl.pallas_call(kernel, out_shape=jax.ShapeDtypeStruct((ROWS, 2 * W, SEQ),...]
where the time goes in v4:
time: 79.8 us; the launch traced here: 79.7 us
  Pallas kernels  79.6 us (100%)
    pallas_call x1, Pallas kernels, shards(): pl.pallas_call(kernel, out_shape=jax.ShapeDtypeStruct((ROWS, 2 * W, SEQ),...  77.3 us
    pallas_call x1, Pallas kernels, shards(): pl.pallas_call(project_out, out_shape=jax.ShapeDtypeStruct((ROWS, SEQ, CH...  2.39 us

profile of v4, /device:TPU:33, one launch (start us, length us, event | category | flops | bytes accessed | tf_op | source)
XLA Modules:
  0.0 79.7 jit_solution(13652354379181521259)
XLA Ops:
  0.0 77.3 %fused.1.lr = bf16[16,64,128]{2,1,0:T(8,128)(2,1)} custom-call(bf16[16,128,256]{2,1,0:T(8,128)(2,1)} %bitcast.14, bf16[32,256]{1,0:T(8,128)(2,1)} %bitcast.10, bf16[32,256]{1,0:T(8,128)(2,1)} %bitcast.12, bf16[1024,128]{1,0:T(8,128)(2,1)} %bitcast.16, bf16[16,4,4,16,128]{4,3,2,1,0:T(8,128)(2,1)} %bitcast.15, f32[1,128]{1,0:T(1,128)} %gain_hbm.1), custom_call_target="tpu_custom_call" | custom-call | flops 3400000000 | bytes 4194304 | tf_op jit(solution)/shard_map/fused/pallas_call | solution.py:445
  77.3 2.4 %project_out.1 = bf16[16,128,256]{2,1,0:T(8,128)(2,1)} custom-call(bf16[16,64,128]{2,1,0:T(8,128)(2,1)} %fused.1.lr, bf16[32,256]{1,0:T(8,128)(2,1)} %bitcast.11, bf16[32,256]{1,0:T(8,128)(2,1)} %bitcast.13), custom_call_target="tpu_custom_call" | custom-call | tf_op jit(solution)/shard_map/project_out/pallas_call | solution.py:510

commit v5 on v4

--- a/solution.py
+++ b/solution.py
@@ -99,7 +99,7 @@
             body(d)
             return 0
 
-        lax.fori_loop(low, high, step, 0)
+        lax.fori_loop(low, high, step, 0, unroll=True)
 
     def send_fwd(c):
         each(lambda d: fwd(c, d).start())
@@ -128,7 +128,7 @@
             rf[pl.ds(rows, W), :] = both[W:, t * SEQ : (t + 1) * SEQ]
         return 0
 
-    lax.fori_loop(0, ROWS // 2, project, 0)
+    lax.fori_loop(0, ROWS // 2, project, 0, unroll=4)
     for y in range(W):
         rall[mx, mz, mc, y] = rf[pl.ds(y, ROWS, stride=W), :].astype(BF)
 
@@ -317,7 +317,7 @@
                     ).astype(BF)
                     return 0
 
-                lax.fori_loop(0, YN, add_core, 0)
+                lax.fori_loop(0, YN, add_core, 0, unroll=4)
                 for d in range(1, NX):
                     x_copy(c, g, d).start()
 
@@ -338,7 +338,7 @@
                     zs[c // 2, y] = total.astype(BF)
                     return 0
 
-                lax.fori_loop(0, YN, add_x, 0)
+                lax.fori_loop(0, YN, add_x, 0, unroll=4)
 
                 @pl.when(mz != c // 2)
                 def _():
@@ -354,7 +354,7 @@
                 rgf[pl.ds(rows, ROWS), :] = zs[mz, y].astype(F32) + zr[y].astype(F32)
                 return 0
 
-            lax.fori_loop(0, YN, add_z, 0)
+            lax.fori_loop(0, YN, add_z, 0, unroll=8)
 
     def sent_fwd():
         for c in range(NQ):
@@ -388,25 +388,25 @@
     scan(2)
     scan(3)
     pass_z()
+    products(0)
     pass_x(0)
-    products(0)
     over_cores(0)
+    products(1)
     pass_x(1)
-    products(1)
     over_x(0)
     over_cores(1)
     products(2)
-    for x in range(NX):
-        for z in range(NZ):
-            arrived(x, z, 1 - mc)
-    left_products(0)
-    left_products(1)
     over_x(1)
     over_cores(2)
     sent_fwd()
     products(3)
     over_x(2)
     over_cores(3)
+    for x in range(NX):
+        for z in range(NZ):
+            arrived(x, z, 1 - mc)
+    left_products(0)
+    left_products(1)
     left_products(2)
     left_products(3)
     for i in range(ROWS):

time: 79.8 us -> 78.2 us (0.980)
  Pallas kernels: 79.6 us -> 78 us
    pallas_call x1, Pallas kernels: 77.3 us -> 75.7 us  [shards(): pl.pallas_call(kernel, out_shape=jax.ShapeDtypeStruct((ROWS, 2 * W, SEQ),...]
where the time goes in v5:
time: 78.2 us; the launch traced here: 78.1 us
  Pallas kernels  78 us (100%)
    pallas_call x1, Pallas kernels, shards(): pl.pallas_call(kernel, out_shape=jax.ShapeDtypeStruct((ROWS, 2 * W, SEQ),...  75.7 us
    pallas_call x1, Pallas kernels, shards(): pl.pallas_call(project_out, out_shape=jax.ShapeDtypeStruct((ROWS, SEQ, CH...  2.39 us

profile of v5, /device:TPU:33, one launch (start us, length us, event | category | flops | bytes accessed | tf_op | source)
XLA Modules:
  0.0 78.1 jit_solution(93624312316769407)
XLA Ops:
  0.0 75.7 %fused.1.lr = bf16[16,64,128]{2,1,0:T(8,128)(2,1)} custom-call(bf16[16,128,256]{2,1,0:T(8,128)(2,1)} %bitcast.14, bf16[32,256]{1,0:T(8,128)(2,1)} %bitcast.10, bf16[32,256]{1,0:T(8,128)(2,1)} %bitcast.12, bf16[1024,128]{1,0:T(8,128)(2,1)} %bitcast.16, bf16[16,4,4,16,128]{4,3,2,1,0:T(8,128)(2,1)} %bitcast.15, f32[1,128]{1,0:T(1,128)} %gain_hbm.1), custom_call_target="tpu_custom_call" | custom-call | flops 3400000000 | bytes 4194304 | tf_op jit(solution)/shard_map/fused/pallas_call | solution.py:445
  75.7 2.4 %project_out.1 = bf16[16,128,256]{2,1,0:T(8,128)(2,1)} custom-call(bf16[16,64,128]{2,1,0:T(8,128)(2,1)} %fused.1.lr, bf16[32,256]{1,0:T(8,128)(2,1)} %bitcast.11, bf16[32,256]{1,0:T(8,128)(2,1)} %bitcast.13), custom_call_target="tpu_custom_call" | custom-call | tf_op jit(solution)/shard_map/project_out/pallas_call | solution.py:510

commit v6 on v5

--- a/solution.py
+++ b/solution.py
@@ -21,7 +21,7 @@
 YP = W // 2
 YG = 4
 YN = W // YG
-STEP = 8
+STEP = 16
 
 
 def kernel(
@@ -400,8 +400,8 @@
     over_cores(2)
     sent_fwd()
     products(3)
+    over_cores(3)
     over_x(2)
-    over_cores(3)
     for x in range(NX):
         for z in range(NZ):
             arrived(x, z, 1 - mc)
@@ -411,17 +411,17 @@
     left_products(3)
     for i in range(ROWS):
         lrv[i, :W] = (lacc[i * W : (i + 1) * W, :] * (1.0 / SEQ)).astype(BF)
+    over_x(NQ - 1)
+    over_z()
+
+    for i in range(ROWS):
+        lrv[i, W:] = (rgf[pl.ds(i, W, stride=ROWS), :] * (1.0 / SEQ)).astype(BF)
+    done = pltpu.make_async_copy(lrv, lr_hbm, out_sem)
+    done.start()
     sent(0)
     sent(1)
     sent(2)
     sent_back()
-    over_x(NQ - 1)
-    over_z()
-
-    for i in range(ROWS):
-        lrv[i, W:] = (rgf[pl.ds(i, W, stride=ROWS), :] * (1.0 / SEQ)).astype(BF)
-    done = pltpu.make_async_copy(lrv, lr_hbm, out_sem)
-    done.start()
     sent(3)
     sent_z()
 

time: 78.2 us -> 78 us (level)
  no operation moved by 1% of the time
where the time goes in v6:
time: 78 us; the launch traced here: 77.9 us
  Pallas kernels  77.9 us (100%)
    pallas_call x1, Pallas kernels, shards(): pl.pallas_call(kernel, out_shape=jax.ShapeDtypeStruct((ROWS, 2 * W, SEQ),...  75.5 us
    pallas_call x1, Pallas kernels, shards(): pl.pallas_call(project_out, out_shape=jax.ShapeDtypeStruct((ROWS, SEQ, CH...  2.41 us

profile of v6, /device:TPU:33, one launch (start us, length us, event | category | flops | bytes accessed | tf_op | source)
XLA Modules:
  0.0 77.9 jit_solution(16360061926113405893)
XLA Ops:
  0.0 75.5 %fused.1.lr = bf16[16,64,128]{2,1,0:T(8,128)(2,1)} custom-call(bf16[16,128,256]{2,1,0:T(8,128)(2,1)} %bitcast.14, bf16[32,256]{1,0:T(8,128)(2,1)} %bitcast.10, bf16[32,256]{1,0:T(8,128)(2,1)} %bitcast.12, bf16[1024,128]{1,0:T(8,128)(2,1)} %bitcast.16, bf16[16,4,4,16,128]{4,3,2,1,0:T(8,128)(2,1)} %bitcast.15, f32[1,128]{1,0:T(1,128)} %gain_hbm.1), custom_call_target="tpu_custom_call" | custom-call | flops 3400000000 | bytes 4194304 | tf_op jit(solution)/shard_map/fused/pallas_call | solution.py:445
  75.5 2.4 %project_out.1 = bf16[16,128,256]{2,1,0:T(8,128)(2,1)} custom-call(bf16[16,64,128]{2,1,0:T(8,128)(2,1)} %fused.1.lr, bf16[32,256]{1,0:T(8,128)(2,1)} %bitcast.11, bf16[32,256]{1,0:T(8,128)(2,1)} %bitcast.13), custom_call_target="tpu_custom_call" | custom-call | tf_op jit(solution)/shard_map/project_out/pallas_call | solution.py:510

commit v7 on v6

--- a/solution.py
+++ b/solution.py
@@ -19,7 +19,7 @@
 NQ = NZ * NC
 JC = NX * ROWS
 YP = W // 2
-YG = 4
+YG = 2
 YN = W // YG
 STEP = 16
 

time: 78 us -> 78.6 us (level)
  no operation moved by 1% of the time
where the time goes in v7:
time: 78.6 us; the launch traced here: 78.5 us
  Pallas kernels  78.5 us (100%)
    pallas_call x1, Pallas kernels, shards(): pl.pallas_call(kernel, out_shape=jax.ShapeDtypeStruct((ROWS, 2 * W, SEQ),...  76.1 us
    pallas_call x1, Pallas kernels, shards(): pl.pallas_call(project_out, out_shape=jax.ShapeDtypeStruct((ROWS, SEQ, CH...  2.41 us

profile of v7, /device:TPU:33, one launch (start us, length us, event | category | flops | bytes accessed | tf_op | source)
XLA Modules:
  0.0 78.5 jit_solution(611265034150038751)
XLA Ops:
  0.0 76.1 %fused.1.lr = bf16[16,64,128]{2,1,0:T(8,128)(2,1)} custom-call(bf16[16,128,256]{2,1,0:T(8,128)(2,1)} %bitcast.14, bf16[32,256]{1,0:T(8,128)(2,1)} %bitcast.10, bf16[32,256]{1,0:T(8,128)(2,1)} %bitcast.12, bf16[1024,128]{1,0:T(8,128)(2,1)} %bitcast.16, bf16[16,4,4,16,128]{4,3,2,1,0:T(8,128)(2,1)} %bitcast.15, f32[1,128]{1,0:T(1,128)} %gain_hbm.1), custom_call_target="tpu_custom_call" | custom-call | flops 3400000000 | bytes 4194304 | tf_op jit(solution)/shard_map/fused/pallas_call | solution.py:445
  76.1 2.4 %project_out.1 = bf16[16,128,256]{2,1,0:T(8,128)(2,1)} custom-call(bf16[16,64,128]{2,1,0:T(8,128)(2,1)} %fused.1.lr, bf16[32,256]{1,0:T(8,128)(2,1)} %bitcast.11, bf16[32,256]{1,0:T(8,128)(2,1)} %bitcast.13), custom_call_target="tpu_custom_call" | custom-call | tf_op jit(solution)/shard_map/project_out/pallas_call | solution.py:510
